TPU v7x, 32 devices: a whole 2x2x4 slice. The times are simulated.
32 devices in a mesh: wave: 16 (over z, y, x), lev: 2 (over core).
Axes of the slice: x: 2, y: 2, z: 4, core: 2. Of those that a mesh axis runs over, the one named last changes fastest.
Arguments:
- fourier_in: bfloat16 [3, 28, 1280, 64], P(None, 'lev', 'wave'), may hold values from -6 to 6
- spectral_old: bfloat16 [3, 28, 16, 2816], P(None, 'lev', 'wave'), may hold values from -6 to 6
- legendre: bfloat16 [16, 1408, 1280], P('wave'), may hold values from -0.15625 to 0.15625
- g_matrix: float32 [28, 28], replicated, may hold values from -1 to 1
- modes_in: float32 [28, 28], replicated, may hold values from -1 to 1
- modes_out: float32 [28, 28], replicated, may hold values from -1 to 1
- mode_heating: float32 [28, 28], replicated, may hold values from -1 to 1
- mode_rates: float32 [28], replicated, may hold values from 0.1 to 10
- pair_ids: int32 [16], replicated, may hold values from 0 to 639, as said below
- lat_ids: int32 [1280], replicated, may hold values from 0 to 1279, each once
- limits: int32 [1280], replicated, may hold values from 10 to 1280
Outputs:
- spectral_new: bfloat16 [3, 28, 16, 2816], P(None, 'lev', 'wave')
- fourier_out: bfloat16 [3, 28, 1280, 64], P(None, 'lev', 'wave')
Inputs may be any that keep to these rules, and one draw needn't show every extreme that they name: `pair_ids`: distinct pair numbers. `lat_ids`: each latitude once.
All inputs are finite; a program needn't handle non-finite values.
Results may differ from a plain program's by a relative error of at most 0.018.
Values may be sent and summed in bfloat16 or wider, within the bound.
A program may use at most 64 MiB of HBM per device.

v0:
```python
import jax
import jax.numpy as jnp
from jax import lax
from jax.sharding import PartitionSpec as P

MMAX = 1280
BLOCK = 64


coupling = 2.0
highest = lax.Precision.HIGHEST


def pair_layout(pair_number, row_count):
    row_index = jnp.arange(row_count, dtype=jnp.int32)
    first_length = MMAX - pair_number
    first_pad = (first_length + BLOCK - 1) // BLOCK * BLOCK
    in_first = row_index < first_pad
    row_valid = jnp.where(
        in_first, row_index < first_length, row_index - first_pad < pair_number + 1
    )
    degree = jnp.where(
        in_first, pair_number + row_index, MMAX - 1 - pair_number + row_index - first_pad
    ).astype(jnp.float32)
    lfactor = degree * (degree + 1.0) / float(MMAX * (MMAX - 1))
    return (row_valid, lfactor, first_pad)


def level_term(matrix, vector, level_start, lev_count, row_start, row_total):
    rows_block = lax.dynamic_slice(
        matrix, (jnp.asarray(row_start, jnp.int32), level_start), (row_total, lev_count)
    )
    return jnp.dot(rows_block, vector, precision=highest, preferred_element_type=jnp.float32)


def legendre_forward(stacked, pair_table, first_pad, pair_number, row_count):
    column_count = stacked.shape[1]

    def block_step(block_index, running, which_wave):
        start_row = block_index * BLOCK
        table_rows = lax.dynamic_slice_in_dim(pair_table, start_row, BLOCK, 0)
        product = lax.dot_general(
            stacked[which_wave],
            table_rows,
            (((1,), (1,)), ((), ())),
            preferred_element_type=jnp.float32,
        )
        return lax.dynamic_update_slice_in_dim(running, product, start_row, 1)

    running = jnp.zeros((column_count, row_count), jnp.float32)
    split_block = first_pad // BLOCK
    end_block = (first_pad + pair_number + BLOCK) // BLOCK
    running = lax.fori_loop(
        0, split_block, lambda block_index, carried: block_step(block_index, carried, 0), running
    )
    running = lax.fori_loop(
        split_block,
        end_block,
        lambda block_index, carried: block_step(block_index, carried, 1),
        running,
    )
    return running


def legendre_inverse(slot_spectra, pair_table, first_pad, pair_number):
    column_count = slot_spectra.shape[0]
    lat_total = pair_table.shape[1]

    def block_step(block_index, running):
        start_row = block_index * BLOCK
        table_rows = lax.dynamic_slice_in_dim(pair_table, start_row, BLOCK, 0)
        spectra_rows = lax.dynamic_slice_in_dim(slot_spectra, start_row, BLOCK, 1)
        return running + jnp.dot(spectra_rows, table_rows, preferred_element_type=jnp.float32)

    zeros_grid = jnp.zeros((column_count, lat_total), jnp.float32)
    split_block = first_pad // BLOCK
    end_block = (first_pad + pair_number + BLOCK) // BLOCK
    first_wave = lax.fori_loop(0, split_block, block_step, zeros_grid)
    second_wave = lax.fori_loop(split_block, end_block, block_step, zeros_grid)
    return jnp.stack([first_wave, second_wave])


def body(
    fourier_in,
    spectral_old,
    legendre,
    g_matrix,
    modes_in,
    modes_out,
    mode_heating,
    mode_rates,
    pair_ids,
    lat_ids,
    limits,
):
    lev_count = fourier_in.shape[1]
    lat_count = fourier_in.shape[2]
    pair_count = legendre.shape[0]
    row_count = legendre.shape[1]
    lat_total = legendre.shape[2]
    wave_index = lax.axis_index("wave")
    level_start = lax.axis_index("lev") * lev_count
    pair_slot = 0
    pair_number = lax.dynamic_slice_in_dim(pair_ids, wave_index * pair_count + pair_slot, 1)[0]
    layouts = [(pair_number,) + pair_layout(pair_number, row_count)]
    own_lats = lax.dynamic_slice_in_dim(lat_ids, wave_index * lat_count, lat_count)
    matches = own_lats[:, None] == jnp.arange(lat_total, dtype=jnp.int32)[None, :]
    row_limit = jnp.sum(jnp.where(matches, limits[None, :], 0), axis=1)
    both_waves = jnp.stack([pair_ids, MMAX - 1 - pair_ids], axis=1)
    column_wave = jnp.repeat(both_waves, 2, axis=1).reshape(-1)
    keep_mask = column_wave[None, :] < row_limit[:, None]
    masked = jnp.where(keep_mask[None, None], fourier_in, jnp.zeros((), fourier_in.dtype))
    exchanged = lax.all_to_all(masked, "wave", split_axis=3, concat_axis=2, tiled=True)
    item_count = exchanged.shape[0]
    column_count = item_count * lev_count * 2
    pair_slot = 0
    pair_number, row_valid, lfactor, first_pad = layouts[pair_slot]
    slot_data = exchanged.reshape(item_count, lev_count, lat_total, 2, 2)
    stacked = jnp.transpose(slot_data, (3, 0, 1, 4, 2)).reshape(2, column_count, lat_total)
    spectra = legendre_forward(stacked, legendre[pair_slot], first_pad, pair_number, row_count)
    spectra = jnp.where(row_valid[None, :], spectra, 0.0)
    results = [spectra.reshape(item_count, lev_count, 2, row_count)]
    tendency = jnp.stack(results, axis=2)
    flat_size = pair_count * 2 * row_count
    old_fields = spectral_old.reshape(3, lev_count, pair_count, 2, row_count).astype(jnp.float32)
    vorticity = (old_fields[0] + tendency[0]).reshape(lev_count, flat_size)
    divergence = (old_fields[1] + tendency[1]).reshape(lev_count, flat_size)
    heat_star = (old_fields[2] + tendency[2]).reshape(lev_count, flat_size)
    wave_factor = jnp.stack(
        [jnp.broadcast_to(layout[2][None, :], (2, row_count)) for layout in layouts]
    ).reshape(1, flat_size)
    keep_rows = jnp.stack(
        [jnp.broadcast_to(layout[1][None, :], (2, row_count)) for layout in layouts]
    ).reshape(1, flat_size)
    rates_own = lax.dynamic_slice_in_dim(mode_rates, level_start, lev_count)
    hydrostatic = lax.psum_scatter(
        level_term(
            g_matrix,
            heat_star,
            level_start,
            lev_count,
            jnp.int32(0),
            lev_count * lax.axis_size("lev"),
        ).astype(jnp.bfloat16),
        "lev",
        scatter_dimension=0,
        tiled=True,
    ).astype(jnp.float32)
    right_own = divergence + coupling * wave_factor * hydrostatic
    projected = lax.psum_scatter(
        level_term(
            modes_in,
            right_own,
            level_start,
            lev_count,
            jnp.int32(0),
            lev_count * lax.axis_size("lev"),
        ).astype(jnp.bfloat16),
        "lev",
        scatter_dimension=0,
        tiled=True,
    ).astype(jnp.float32)
    modal_part = projected / (1.0 + coupling * coupling * wave_factor * rates_own[:, None])
    row_start = jnp.int32(0)
    row_total = lev_count * lax.axis_size("lev")
    divergence_part = level_term(
        modes_out, modal_part, level_start, lev_count, row_start, row_total
    )
    heating_part = level_term(
        mode_heating, modal_part, level_start, lev_count, row_start, row_total
    )
    rebuilt = lax.psum_scatter(
        jnp.stack([divergence_part, heating_part], axis=1).astype(jnp.bfloat16),
        "lev",
        scatter_dimension=0,
        tiled=True,
    ).astype(jnp.float32)
    vorticity_out = jnp.where(keep_rows, vorticity, 0.0).astype(jnp.bfloat16)
    divergence_out = jnp.where(keep_rows, rebuilt[:, 0], 0.0).astype(jnp.bfloat16)
    heat_out = jnp.where(keep_rows, heat_star - coupling * rebuilt[:, 1], 0.0).astype(jnp.bfloat16)
    spectral_new = jnp.stack([vorticity_out, divergence_out, heat_out]).reshape(
        3, lev_count, pair_count, 2 * row_count
    )
    pair_slot = 0
    pair_number, row_valid, lfactor, first_pad = layouts[pair_slot]
    slot_spectra = spectral_new[:, :, pair_slot].reshape(3 * lev_count * 2, row_count)
    grid_part = legendre_inverse(slot_spectra, legendre[pair_slot], first_pad, pair_number)
    grid_part = (
        grid_part.reshape(2, 3, lev_count, 2, lat_total)
        .transpose(1, 2, 4, 0, 3)
        .reshape(3, lev_count, lat_total, 4)
    )
    gridded = grid_part.astype(jnp.bfloat16)
    returned = lax.all_to_all(gridded, "wave", split_axis=2, concat_axis=3, tiled=True)
    fourier_out = jnp.where(keep_mask[None, None], returned, jnp.zeros((), jnp.bfloat16))
    return (spectral_new, fourier_out)


def solution(mesh):
    placed = (
        P(None, "lev", "wave", None),
        P(None, "lev", "wave", None),
        P("wave", None, None),
        P(),
        P(),
        P(),
        P(),
        P(),
        P(),
        P(),
        P(),
    )
    return jax.shard_map(
        body,
        mesh=mesh,
        in_specs=placed,
        out_specs=(P(None, "lev", "wave", None), P(None, "lev", "wave", None)),
        check_vma=False,
    )
```

profile of v0, /device:TPU:0, one launch (start us, length us, event | category | flops | bytes accessed | tf_op | source)
XLA Modules:
  0.0 189.5 jit_solution(12464096708221175484)
XLA Ops:
  11.8 1.3 copy.81
  13.1 8.3 %all-to-all-start = ((bf16[3,14,80,64]{2,1,0,3:T(8,128)(2,1)}), bf16[3,14,80,64]{2,1,0,3:T(8,128)(2,1)S(1)}, u32[]{:S(2)}, u32[]{:S(2)}) async-start(bf16[3,14,80,64]{2,1,0,3:T(8,128)(2,1)} %copy.81), calls=%async_computation | async-start | bytes 1572864 | tf_op jit(solution)/shard_map/all_to_all | solution.py:113
  25.5 15.7 %all-to-all-done = bf16[3,14,80,64]{2,1,0,3:T(8,128)(2,1)S(1)} async-done(((bf16[3,14,80,64]{2,1,0,3:T(8,128)(2,1)}), bf16[3,14,80,64]{2,1,0,3:T(8,128)(2,1)S(1)}, u32[]{:S(2)}, u32[]{:S(2)}) %all-to-all-start) | async-done | bytes 430112 | tf_op jit(solution)/shard_map/all_to_all | solution.py:113
  43.2 19.2 %while.40 = (s32[]{:T(128)}, f32[84,1408]{0,1:T(8,128)S(1)}, s32[]{:T(128)}, bf16[1408,1280]{1,0:T(8,128)(2,1)}, bf16[2,84,1280]{2,1,0:T(8,128)(2,1)S(1)}, /*index=5*/s32[]{:T(128)}, s32[]{:T(128)}, s32[]{:T(128)}, s32[]{:T(128)}) while((s32[]{:T(128)}, f32[84,1408]{0,1:T(8,128)S(1)}, s32[]{:T(128)}, bf16[1408,1280]{1,0:T(8,128)(2,1)}, ...), condition=%wide.region_2.3_spmd, body=%wide.region_1.2_spmd.sunk | while | flops 13762566 | bytes 423051 | solution.py:53
  62.4 4.5 %while.41 = (s32[]{:T(128)}, f32[84,1408]{0,1:T(8,128)S(1)}, s32[]{:T(128)}, bf16[1408,1280]{1,0:T(8,128)(2,1)}, bf16[2,84,1280]{2,1,0:T(8,128)(2,1)S(1)}, /*index=5*/s32[]{:T(128)}, s32[]{:T(128)}, s32[]{:T(128)}, s32[]{:T(128)}) while((s32[]{:T(128)}, f32[84,1408]{0,1:T(8,128)S(1)}, s32[]{:T(128)}, bf16[1408,1280]{1,0:T(8,128)(2,1)}, ...), condition=%wide.region_4.5_spmd, body=%wide.region_3.4_spmd.sunk | while | flops 13762566 | bytes 423051 | solution.py:56
  68.6 3.0 %fusion = bf16[16,2816]{1,0:T(8,128)(2,1)S(1)} fusion(bf16[28,2816]{1,0:T(8,128)(2,1)S(1)} %convolution_convert_fusion.3), kind=kCustom, calls=%all-reduce-scatter | all-reduce-scatter fusion | flops 90113 | bytes 248320
  71.6 2.3 %collective-permute-start = (bf16[2,2816]{1,0:T(2,128)(2,1)S(1)}, bf16[2,2816]{1,0:T(2,128)(2,1)S(1)}, u32[]{:S(2)}, u32[]{:S(2)}) collective-permute-start(bf16[2,2816]{1,0:T(2,128)(2,1)S(1)} %slice.52), channel_id=1, source_target_pairs={{0,1},{2,3},{4,5},{6,7},{8,9},{10,11},{12,13},{14,15},{16,17},{18,... | collective-permute-start | bytes 33800
  76.9 3.0 %fusion.1 = bf16[16,2816]{1,0:T(8,128)(2,1)S(1)} fusion(bf16[28,2816]{1,0:T(8,128)(2,1)S(1)} %convolution_convert_fusion.2), kind=kCustom, calls=%all-reduce-scatter.1 | all-reduce-scatter fusion | flops 90113 | bytes 248320
  80.0 2.3 %collective-permute-start.1 = (bf16[2,2816]{1,0:T(2,128)(2,1)S(1)}, bf16[2,2816]{1,0:T(2,128)(2,1)S(1)}, u32[]{:S(2)}, u32[]{:S(2)}) collective-permute-start(bf16[2,2816]{1,0:T(2,128)(2,1)S(1)} %slice.53), channel_id=1, source_target_pairs={{0,1},{2,3},{4,5},{6,7},{8,9},{10,11},{12,13},{14,15},{16,17},{18,... | collective-permute-start | bytes 33800
  86.6 16.7 %all-reduce.7.cloned.1.call-done = bf16[28,2,2816]{2,1,0:T(2,128)(2,1)} async-done(((bf16[28,2,2816]{2,1,0:T(2,128)(2,1)}), bf16[28,2,2816]{2,1,0:T(2,128)(2,1)}) %all-reduce.7.cloned.1.call-update) | async-done | bytes 315408
  105.4 4.9 %while.43 = (s32[]{:T(128)}, f32[84,1280]{1,0:T(8,128)S(1)}, s32[]{:T(128)}, bf16[84,1408]{1,0:T(8,128)(2,1)S(1)}, bf16[1408,1280]{1,0:T(8,128)(2,1)}, /*index=5*/s32[]{:T(128)}, s32[]{:T(128)}, s32[]{:T(128)}, s32[]{:T(128)}) while((s32[]{:T(128)}, f32[84,1280]{1,0:T(8,128)S(1)}, s32[]{:T(128)}, bf16[84,1408]{1,0:T(8,128)(2,1)S(1)}, ...), condition=%wide.region_11.12_spmd, body=%wide.region_10.11_spmd.sunk | while | flops 13870086 | bytes 1068171 | solution.py:79
  106.6 1.2 convolution_add_fusion.5
  109.1 1.2 convolution_add_fusion.5
  110.4 20.7 %while.42 = (s32[]{:T(128)}, f32[84,1280]{1,0:T(8,128)S(1)}, s32[]{:T(128)}, bf16[84,1408]{1,0:T(8,128)(2,1)S(1)}, bf16[1408,1280]{1,0:T(8,128)(2,1)}, /*index=5*/s32[]{:T(128)}, s32[]{:T(128)}, s32[]{:T(128)}, s32[]{:T(128)}) while((s32[]{:T(128)}, f32[84,1280]{1,0:T(8,128)S(1)}, s32[]{:T(128)}, bf16[84,1408]{1,0:T(8,128)(2,1)S(1)}, ...), condition=%wide.region_9.10_spmd, body=%wide.region_8.9_spmd.sunk | while | flops 13870086 | bytes 1068171 | solution.py:78
  110.5 1.2 convolution_add_fusion.4
  111.7 1.2 convolution_add_fusion.4
  112.9 1.2 convolution_add_fusion.4
  114.1 1.2 convolution_add_fusion.4
  115.3 1.2 convolution_add_fusion.4
  117.8 1.2 convolution_add_fusion.4
  119.0 1.2 convolution_add_fusion.4
  120.2 1.2 convolution_add_fusion.4
  122.6 1.2 convolution_add_fusion.4
  125.1 1.2 convolution_add_fusion.4
  127.5 1.2 convolution_add_fusion.4
  128.7 1.2 convolution_add_fusion.4
  129.9 1.2 convolution_add_fusion.4
  131.9 6.4 %copy.98 = bf16[3,14,1280,2,2]{1,4,3,0,2:T(2,128)(2,1)} copy(bf16[3,14,1280,2,2]{2,4,3,1,0:T(2,128)(2,1)S(1)} %maximum_bitcast_fusion) | data formatting | bytes 860160 | tf_op jit(solution)/shard_map/convert_element_type | solution.py:193
  138.3 6.7 %reshape.298 = bf16[16,2,6720]{2,1,0:T(2,128)(2,1)S(1)} reshape(bf16[1280,3,4,14]{3,2,1,0:T(4,128)(2,1)} %bitcast.96) | data formatting | bytes 860160
  145.0 20.5 %all_to_all.33 = bf16[16,2,6720]{2,1,0:T(2,128)(2,1)S(1)} all-to-all(bf16[16,2,6720]{2,1,0:T(2,128)(2,1)S(1)} %reshape.298), channel_id=1, replica_groups=mesh['wave'=16,'lev'=2] {'wave'}, dimensions={0} | all-to-all | bytes 860160 | tf_op jit(solution)/shard_map/all_to_all | solution.py:194
  165.5 10.5 %reshape.299 = bf16[1280,3,4,14]{3,2,1,0:T(4,128)(2,1)} reshape(bf16[16,2,6720]{2,1,0:T(2,128)(2,1)S(1)} %all_to_all.33) | data formatting | bytes 860160
  175.9 5.5 %copy.99 = bf16[3,14,16,80,4]{3,2,4,1,0:T(8,128)(2,1)S(1)} copy(bf16[3,14,16,80,4]{1,4,0,3,2:T(4,128)(2,1)} %bitcast.97) | data formatting | bytes 860160 | tf_op jit(solution)/shard_map/all_to_all | solution.py:194
  (107 shorter events, 49.2 us)
Async XLA Ops:
  7.2 60.9 %copy-start = (f32[28,28]{1,0:T(8,128)S(1)}, f32[28,28]{1,0:T(8,128)}, u32[]{:S(2)}) copy-start(f32[28,28]{1,0:T(8,128)} %param.22) | copy-start | bytes 9412
  7.2 14.3 %copy-start.4 = (s32[16]{0:T(128)S(1)}, s32[16]{0:T(128)}, u32[]{:S(2)}) copy-start(s32[16]{0:T(128)} %param.27) | copy-start | bytes 196
  7.2 18.2 %copy-start.1 = (bf16[3,14,1,2816]{3,1,2,0:T(8,128)(2,1)S(1)}, bf16[3,14,1,2816]{3,1,2,0:T(8,128)(2,1)}, u32[]{:S(2)}) copy-start(bf16[3,14,1,2816]{3,1,2,0:T(8,128)(2,1)} %param.20) | copy-start | bytes 709636
  13.1 28.1 %all-to-all-start = ((bf16[3,14,80,64]{2,1,0,3:T(8,128)(2,1)}), bf16[3,14,80,64]{2,1,0,3:T(8,128)(2,1)S(1)}, u32[]{:S(2)}, u32[]{:S(2)}) async-start(bf16[3,14,80,64]{2,1,0,3:T(8,128)(2,1)} %copy.81), calls=%async_computation | async-start | bytes 1572864 | tf_op jit(solution)/shard_map/all_to_all | solution.py:113
  21.5 81.9 %all-reduce.7.cloned.1.call-start = ((), (), s32[]{:S(2)}) async-start(), calls=%async_computation.2 | async-start | bytes 630784
  67.0 7.6 %copy-start.3 = (u32[32]{0:T(128)S(1)}, u32[32]{0:T(128)}, u32[]{:S(2)}) copy-start(u32[32]{0:T(128)} %constant.117) | copy-start | bytes 388
  67.2 9.2 %copy-start.2 = (f32[28,28]{1,0:T(8,128)S(1)}, f32[28,28]{1,0:T(8,128)}, u32[]{:S(2)}) copy-start(f32[28,28]{1,0:T(8,128)} %param.23) | copy-start | bytes 9412
  67.3 15.0 %copy-start.7 = (f32[28]{0:T(128)S(1)}, f32[28]{0:T(128)}, u32[]{:S(2)}) copy-start(f32[28]{0:T(128)} %param.26) | copy-start | bytes 340
  67.3 16.1 %copy-start.5 = (f32[28,28]{1,0:T(8,128)S(1)}, f32[28,28]{1,0:T(8,128)}, u32[]{:S(2)}) copy-start(f32[28,28]{1,0:T(8,128)} %param.25) | copy-start | bytes 9412
  67.7 16.1 %copy-start.6 = (f32[28,28]{1,0:T(8,128)S(1)}, f32[28,28]{1,0:T(8,128)}, u32[]{:S(2)}) copy-start(f32[28,28]{1,0:T(8,128)} %param.24) | copy-start | bytes 9412
  71.6 4.5 %collective-permute-start = (bf16[2,2816]{1,0:T(2,128)(2,1)S(1)}, bf16[2,2816]{1,0:T(2,128)(2,1)S(1)}, u32[]{:S(2)}, u32[]{:S(2)}) collective-permute-start(bf16[2,2816]{1,0:T(2,128)(2,1)S(1)} %slice.52), channel_id=1, source_target_pairs={{0,1},{2,3},{4,5},{6,7},{8,9},{10,11},{12,13},{14,15},{16,17},{18,... | collective-permute-start | bytes 33800
  80.0 3.1 %collective-permute-start.1 = (bf16[2,2816]{1,0:T(2,128)(2,1)S(1)}, bf16[2,2816]{1,0:T(2,128)(2,1)S(1)}, u32[]{:S(2)}, u32[]{:S(2)}) collective-permute-start(bf16[2,2816]{1,0:T(2,128)(2,1)S(1)} %slice.53), channel_id=1, source_target_pairs={{0,1},{2,3},{4,5},{6,7},{8,9},{10,11},{12,13},{14,15},{16,17},{18,... | collective-permute-start | bytes 33800
Sparse Core Ops, SparseCore 0:
  85.6 17.6 all-reduce.6
where the time goes:
time: 191 us; the launch traced here: 190 us
  matrix products  50.2 us (26%)
  local copies, waits for them, and re-layouts  39.6 us (21%)
  waiting for transfers between devices  33.2 us (17%)
  blocking collectives  26.5 us (14%)
  between operations  19.2 us (10%)
  starting transfers between devices  12.9 us (7%)
  other arithmetic  6.88 us (4%)
    dot_general x21, matrix products, block_step(): jnp.dot(spectra_rows, table_rows, preferred_element_type=jnp.float32)  25 us
    dot_general x21, matrix products, block_step(): lax.dot_general(stacked[which_wave], table_rows, (((1,), (1,)), ((), ()))...  23.2 us
    all_to_all x1, blocking collectives, body(): lax.all_to_all(gridded, 'wave', split_axis=2, concat_axis=3, tiled=True)  20.5 us
    unnamed x24, local copies, waits for them, and re-layouts  19.4 us
    unnamed x4, waiting for transfers between devices  17.5 us
    all_to_all x1, waiting for transfers between devices, body(): lax.all_to_all(masked, 'wave', split_axis=3, concat_axis=2, tiled=True)  15.7 us
    all_to_all x1, starting transfers between devices, body(): lax.all_to_all(masked, 'wave', split_axis=3, concat_axis=2, tiled=True)  8.3 us
    convert_element_type x1, local copies, waits for them, and re-layouts, body(): gridded = grid_part.astype(jnp.bfloat16)  6.42 us
  transfers between devices with their start and end apart: 4, of which 3 were waited for; matrix products, arithmetic and copies ran while one was open for 1% of the time, Pallas kernels for 0%

commit v1 on v0

v1 whole, which is shorter than its diff:
```python
import functools

import jax
import jax.numpy as jnp
from jax import lax
from jax.experimental import pallas as pl
from jax.experimental.pallas import tpu as pltpu
from jax.sharding import PartitionSpec as P

MMAX = 1280
BLOCK = 64
K = 4
F32, BF16 = jnp.float32, jnp.bfloat16
MESH = pl.DeviceIdType.MESH
HI = lax.Precision.HIGHEST
NT = (((1,), (1,)), ((), ()))


def iota(shape, dim):
    return lax.broadcasted_iota(jnp.int32, shape, dim)


def dot(a, b):
    return jnp.dot(a, b, preferred_element_type=F32)


def fdot(a, b):
    return jnp.dot(a, b, precision=HI, preferred_element_type=F32)


def onehot(mask, dtype=BF16):
    return jnp.where(mask, 1.0, 0.0).astype(dtype)


def split3(left, right):
    lh = left.astype(BF16)
    ll = (left - lh.astype(F32)).astype(BF16)
    rh = right.astype(BF16)
    rl = (right - rh.astype(F32)).astype(BF16)
    return jnp.concatenate([lh, lh, ll], axis=1), jnp.concatenate([rh, rl, rh], axis=0)


def kernel(
    n, nlev, x_ref, old_ref, leg_hbm, g_ref, mi_ref, mo_ref, mh_ref, rates_ref, pid_ref, lat_ref, lim_ref,
    spec_ref, out_ref,
    leg, send1, recv1, send2, recv2, es1, er1, es2, er2,
    leg_sem, s1, r1, s2, r2, es, er,
):
    lev_n = x_ref.shape[1]
    fl_n = x_ref.shape[0] * lev_n
    q_n, jl = x_ref.shape[2], x_ref.shape[3]
    groups = (fl_n + K - 1) // K
    rows = groups * 16
    trows = groups * 8
    lanes = send1.shape[2]
    nr = leg_hbm.shape[1]
    nlat = leg_hbm.shape[2]
    first_mid = lev_n // K * 8
    mid = trows - first_mid
    half = er1.shape[0]
    me, lev = lax.axis_index("wave"), lax.axis_index("lev")
    other = lax.rem(lev + 1, nlev)

    leg_copy = pltpu.make_async_copy(leg_hbm.at[0], leg, leg_sem)
    leg_copy.start()

    barrier = pltpu.get_barrier_semaphore()

    def greet(i, carry):
        pl.semaphore_signal(barrier, inc=1, device_id=(lax.rem(me + i, n), lev), device_id_type=MESH)
        return carry

    lax.fori_loop(1, n, greet, 0)
    pl.semaphore_signal(barrier, inc=1, device_id=(me, other), device_id_type=MESH)

    col = iota((jl, nlat), 1)
    own = jnp.sum(jnp.where(col == me * jl + iota((jl, nlat), 0), lat_ref[...], 0.0), axis=1, keepdims=True)
    lim = jnp.sum(jnp.where(col.astype(F32) == own, lim_ref[...], 0.0), axis=1, keepdims=True)
    lim = jnp.sum(jnp.where(iota((jl, jl), 0) == iota((jl, jl), 1), lim, 0.0), axis=0, keepdims=True)
    q = iota((q_n, jl), 0)
    slot = q // 4
    pair = jnp.zeros((q_n, jl), jnp.int32)
    for s in range(n):
        pair = jnp.where(slot == s, pid_ref[s], pair)
    wave = jnp.where(q // 2 % 2 == 0, pair, MMAX - 1 - pair)
    keep = onehot(wave.astype(F32) < lim, F32)

    pr, pc = iota((K * q_n, K * q_n), 0), iota((K * q_n, K * q_n), 1)
    perm = onehot(pc == pr % K * q_n + pr // K)
    keep_b = keep.astype(BF16)
    pieces = []
    for k in range(K):
        parts = []
        for g in range(groups):
            fl = g * K + k
            if fl < fl_n:
                parts.append(x_ref[fl // lev_n, fl % lev_n] * keep_b)
            else:
                parts.append(jnp.zeros((q_n, jl), BF16))
        if lanes > groups * jl:
            parts.append(jnp.zeros((q_n, lanes - groups * jl), BF16))
        pieces.append(jnp.concatenate(parts, axis=1))
    send1[...] = dot(perm, jnp.concatenate(pieces, axis=0)).astype(BF16).reshape(n, 16, lanes)

    pl.semaphore_wait(barrier, n)

    def copy1(i):
        to = lax.rem(me + i, n)
        return pltpu.make_async_remote_copy(
            src_ref=send1.at[to], dst_ref=recv1.at[me], send_sem=s1.at[to], recv_sem=r1.at[me],
            device_id=(to, lev), device_id_type=MESH,
        )

    def start1(i, carry):
        copy1(i).start()
        return carry

    lax.fori_loop(1, n, start1, 0)
    recv1[me] = send1[me]

    a = pid_ref[me]
    r = iota((1, nr), 1)
    first_pad = (MMAX - a + BLOCK - 1) // BLOCK * BLOCK
    first = r < first_pad
    used = (first & (r < MMAX - a)) | ((r >= first_pad) & (r - first_pad <= a))
    degree = jnp.where(first, a + r, MMAX - 1 - a + r - first_pad).astype(F32)
    lam = degree * (degree + 1.0) / float(MMAX * (MMAX - 1))

    tr, tc = iota((trows, fl_n), 0), iota((trows, fl_n), 1)
    tfl = tr // 8 * K + tr % K
    old = jnp.concatenate([old_ref[f, 0] for f in range(3)], axis=0)
    old_rows = sum(
        dot(onehot((tfl == tc) & (tr // 4 % 2 == c)), old[:, c * nr : (c + 1) * nr]) for c in range(2)
    )

    def mid_row(i):
        i = i + first_mid
        fl = i // 8 * K + i % K
        return fl // lev_n, fl % lev_n, i // 4 % 2

    levels = nlev * lev_n

    def mode_of(i, h):
        return lev_n * ((lev + h) % nlev) + i // 2

    i1, o1 = iota((2 * half, levels), 0), iota((2 * half, levels), 1)
    pick_out = onehot((o1 == mode_of(i1 % half, i1 // half)) & (i1 % half < 2 * lev_n), F32)
    field, level, cc = mid_row(iota((levels, mid), 1))
    pick_in = onehot(iota((levels, mid), 0) == lev_n * lev + level, F32)
    field, level, cc = mid_row(iota((2 * half, mid), 1))
    same_c = iota((2 * half, mid), 0) % 2 == cc
    m_in = mi_ref[...]
    w_div = jnp.where(same_c & (field == 1), fdot(fdot(pick_out, m_in), pick_in), 0.0)
    w_heat = jnp.where(same_c & (field == 2), fdot(fdot(pick_out, fdot(m_in, g_ref[...])), pick_in), 0.0)
    w1 = jnp.concatenate([w_div, w_heat], axis=0)
    im, om = iota((half, levels), 0), iota((half, levels), 1)
    own_mode = (om == lev_n * lev + im // 2) & (im < 2 * lev_n)
    rates = jnp.sum(jnp.where(own_mode, rates_ref[...], 0.0), axis=1, keepdims=True)
    i2, l2 = iota((2 * mid, levels), 0), iota((2 * mid, levels), 1)
    field, level, cc = mid_row(i2 % mid)
    pick_lev = onehot(l2 == lev_n * ((lev + i2 // mid) % nlev) + level, F32)
    im, om = iota((levels, half), 1), iota((levels, half), 0)
    pick_mode = onehot((om == lev_n * lev + im // 2) & (im < 2 * lev_n), F32)
    field, level, cc = mid_row(iota((2 * mid, half), 0) % mid)
    same_c = iota((2 * mid, half), 1) % 2 == cc
    w2 = jnp.where(same_c & (field == 1), fdot(fdot(pick_lev, mo_ref[...]), pick_mode), 0.0)
    w2 = w2 + jnp.where(same_c & (field == 2), -2.0 * fdot(fdot(pick_lev, mh_ref[...]), pick_mode), 0.0)
    field, level, cc = mid_row(iota((mid, 1), 0))
    stays = onehot(field != 1, F32)

    leg_copy.wait()

    def wait1(i, carry):
        copy1(i).wait_send()
        frm = lax.rem(me + n - i, n)
        pltpu.make_async_remote_copy(
            src_ref=send1.at[frm], dst_ref=recv1.at[frm], send_sem=s1.at[frm], recv_sem=r1.at[frm],
            device_id=(frm, lev), device_id_type=MESH,
        ).wait_recv()
        return carry

    lax.fori_loop(1, n, wait1, 0)

    cols = jnp.concatenate(
        [
            jnp.concatenate([recv1[d, :, g * jl : (g + 1) * jl] for d in range(n)], axis=1)
            for g in range(groups)
        ],
        axis=0,
    )
    both = lax.dot_general(cols, leg[...], NT, preferred_element_type=F32).reshape(groups, 2, 8, nr)
    total = jnp.where(iota((groups, 8, nr), 2) < first_pad, both[:, 0], both[:, 1])
    total = old_rows + jnp.where(used, total.reshape(trows, nr), 0.0)

    def exchange(src, dst, k):
        return pltpu.make_async_remote_copy(
            src_ref=src, dst_ref=dst, send_sem=es.at[k], recv_sem=er.at[k],
            device_id=(me, other), device_id_type=MESH,
        )

    tmid = total[first_mid:]
    w1s, t1s = split3(w1, tmid)
    res = dot(w1s, t1s)
    proj = res[: 2 * half] + 2.0 * lam * res[2 * half :]
    es1[...] = proj[half:].astype(BF16)
    exchange(es1, er1, 0).start()
    exchange(es1, er1, 0).wait()
    modal = (proj[:half] + er1[...].astype(F32)) / (1.0 + 4.0 * lam * rates)
    w2s, m2s = split3(w2, modal)
    res = dot(w2s, m2s)
    es2[...] = res[mid:].astype(BF16)
    exchange(es2, er2, 1).start()
    exchange(es2, er2, 1).wait()
    new_mid = tmid * stays + res[:mid] + er2[...].astype(F32)
    new = jnp.concatenate([total[:first_mid], new_mid], axis=0) if first_mid else new_mid
    new = jnp.where(used, new, 0.0)
    sides = jnp.stack(
        [
            jnp.where(first, new, 0.0).reshape(groups, 8, nr),
            jnp.where(first, 0.0, new).reshape(groups, 8, nr),
        ],
        axis=1,
    ).reshape(rows, nr).astype(BF16)
    grid = dot(sides, leg[...]).astype(BF16)
    for d in range(n):
        parts = [grid[g * 16 : (g + 1) * 16, d * jl : (d + 1) * jl] for g in range(groups)]
        if lanes > groups * jl:
            parts.append(jnp.zeros((16, lanes - groups * jl), BF16))
        send2[d] = jnp.concatenate(parts, axis=1)

    def copy2(i):
        to = lax.rem(me + i, n)
        return pltpu.make_async_remote_copy(
            src_ref=send2.at[to], dst_ref=recv2.at[me], send_sem=s2.at[to], recv_sem=r2.at[me],
            device_id=(to, lev), device_id_type=MESH,
        )

    def start2(i, carry):
        copy2(i).start()
        return carry

    lax.fori_loop(1, n, start2, 0)
    recv2[me] = send2[me]

    new_b = new.astype(BF16)
    sr, sc = iota((fl_n, trows), 0), iota((fl_n, trows), 1)
    sfl = sc // 8 * K + sc % K
    for c in range(2):
        part = dot(onehot((sfl == sr) & (sc // 4 % 2 == c)), new_b).astype(BF16)
        for f in range(3):
            spec_ref[f, 0, :, c * nr : (c + 1) * nr] = part[f * lev_n : (f + 1) * lev_n]

    def wait2(i, carry):
        copy2(i).wait_send()
        frm = lax.rem(me + n - i, n)
        pltpu.make_async_remote_copy(
            src_ref=send2.at[frm], dst_ref=recv2.at[frm], send_sem=s2.at[frm], recv_sem=r2.at[frm],
            device_id=(frm, lev), device_id_type=MESH,
        ).wait_recv()
        return carry

    lax.fori_loop(1, n, wait2, 0)
    perm_back = onehot(pr == pc % K * q_n + pc // K)
    back = dot(perm_back, recv2[...].reshape(K * q_n, lanes))
    for g in range(groups):
        for k in range(K):
            fl = g * K + k
            if fl < fl_n:
                piece = back[k * q_n : (k + 1) * q_n, g * jl : (g + 1) * jl] * keep
                out_ref[fl // lev_n, fl % lev_n] = piece.astype(BF16)


def body(
    fourier_in, spectral_old, legendre, g_matrix, modes_in, modes_out, mode_heating, mode_rates, pair_ids, lat_ids,
    limits,
):
    n, nlev = lax.axis_size("wave"), lax.axis_size("lev")
    fields, lev_n, jl, q_n = fourier_in.shape
    groups = (fields * lev_n + K - 1) // K
    lanes = (groups * jl + 127) // 128 * 128
    nr, nlat = legendre.shape[1:]
    half = (2 * lev_n + 15) // 16 * 16
    mid = groups * 8 - lev_n // K * 8
    vmem = pl.BlockSpec(memory_space=pltpu.VMEM)
    spec, out = pl.pallas_call(
        functools.partial(kernel, n, nlev),
        out_shape=(
            jax.ShapeDtypeStruct((fields, 1, lev_n, 2 * nr), BF16),
            jax.ShapeDtypeStruct((fields, lev_n, q_n, jl), BF16),
        ),
        in_specs=[vmem, vmem, pl.BlockSpec(memory_space=pl.ANY)] + [vmem] * 5
        + [pl.BlockSpec(memory_space=pltpu.SMEM)] + [vmem] * 2,
        out_specs=(vmem, vmem),
        scratch_shapes=[
            pltpu.VMEM((nr, nlat), BF16),
            pltpu.VMEM((n, 16, lanes), BF16),
            pltpu.VMEM((n, 16, lanes), BF16),
            pltpu.VMEM((n, 16, lanes), BF16),
            pltpu.VMEM((n, 16, lanes), BF16),
            pltpu.VMEM((half, nr), BF16),
            pltpu.VMEM((half, nr), BF16),
            pltpu.VMEM((mid, nr), BF16),
            pltpu.VMEM((mid, nr), BF16),
            pltpu.SemaphoreType.DMA,
            pltpu.SemaphoreType.DMA((n,)),
            pltpu.SemaphoreType.DMA((n,)),
            pltpu.SemaphoreType.DMA((n,)),
            pltpu.SemaphoreType.DMA((n,)),
            pltpu.SemaphoreType.DMA((2,)),
            pltpu.SemaphoreType.DMA((2,)),
        ],
        compiler_params=pltpu.CompilerParams(
            collective_id=0, has_side_effects=True, vmem_limit_bytes=48 * 1024 * 1024
        ),
        cost_estimate=pl.CostEstimate(flops=10**9, bytes_accessed=8 * 10**6, transcendentals=0),
    )(
        jnp.transpose(fourier_in, (0, 1, 3, 2)),
        jnp.transpose(spectral_old, (0, 2, 1, 3)),
        legendre,
        g_matrix,
        modes_in,
        modes_out,
        mode_heating,
        mode_rates[None, :],
        pair_ids,
        lat_ids.astype(F32)[None, :],
        limits.astype(F32)[None, :],
    )
    return jnp.transpose(spec, (0, 2, 1, 3)), jnp.transpose(out, (0, 1, 3, 2))


def solution(mesh):
    wave = P(None, "lev", "wave", None)
    return jax.shard_map(
        body,
        mesh=mesh,
        in_specs=(wave, wave, P("wave", None, None)) + (P(),) * 8,
        out_specs=(wave, wave),
        check_vma=False,
    )
```

time: 191 us -> 47.1 us (0.25)
  the two profiles are of different devices: /device:TPU:0 before, /device:TPU:28 now
where the time goes in v1:
time: 47.1 us; the launch traced here: 46.4 us
  Pallas kernels  34.5 us (73%)
  local copies, waits for them, and re-layouts  9.82 us (21%)
  other arithmetic  1.4 us (3%)
  between operations  0.65 us (1%)
    pallas_call x1, Pallas kernels, body(): pl.pallas_call(functools.partial(kernel, n, nlev), out_shape=(jax.ShapeDt...  34.5 us
    unnamed x20, local copies, waits for them, and re-layouts  9.8 us

profile of v1, /device:TPU:28, one launch (start us, length us, event | category | flops | bytes accessed | tf_op | source)
XLA Modules:
  0.0 46.4 jit_solution(18390114223472677960)
XLA Ops:
  0.6 0.7 %convert_element_type.6 = f32[1280]{0:T(1024)S(1)} convert(s32[1280]{0:T(1024)} %param.20) | non-fusion elementwise | flops 1280 | bytes 10240 | tf_op jit(solution)/shard_map/convert_element_type | solution.py:326
  1.3 0.7 %convert_element_type.7 = f32[1280]{0:T(1024)S(1)} convert(s32[1280]{0:T(1024)} %param.21) | non-fusion elementwise | flops 1280 | bytes 10240 | tf_op jit(solution)/shard_map/convert_element_type | solution.py:327
  2.0 0.0 copy-start
  2.0 2.0 %copy-done = bf16[1,1408,1280]{2,1,0:T(8,128)(2,1)S(1)} copy-done((bf16[1,1408,1280]{2,1,0:T(8,128)(2,1)S(1)}, bf16[1,1408,1280]{2,1,0:T(8,128)(2,1)}, u32[]{:S(2)}) %copy-start) | copy-done | bytes 3604504
  4.1 0.0 copy-start.1
  4.1 1.1 %copy-done.1 = bf16[3,14,80,64]{2,3,1,0:T(8,128)(2,1)S(1)} copy-done((bf16[3,14,80,64]{2,3,1,0:T(8,128)(2,1)S(1)}, bf16[3,14,80,64]{2,3,1,0:T(8,128)(2,1)}, u32[]{:S(2)}) %copy-start.1) | copy-done | bytes 430104
  5.2 0.0 copy-start.2
  5.2 1.0 %copy-done.2 = bf16[3,14,1,2816]{3,1,2,0:T(8,128)(2,1)S(1)} copy-done((bf16[3,14,1,2816]{3,1,2,0:T(8,128)(2,1)S(1)}, bf16[3,14,1,2816]{3,1,2,0:T(8,128)(2,1)}, u32[]{:S(2)}) %copy-start.2) | copy-done | bytes 236568
  6.1 0.0 copy-start.3
  6.1 0.7 %copy-done.3 = f32[28,28]{1,0:T(8,128)S(1)} copy-done((f32[28,28]{1,0:T(8,128)S(1)}, f32[28,28]{1,0:T(8,128)}, u32[]{:S(2)}) %copy-start.3) | copy-done | bytes 3160
  6.8 0.0 copy-start.4
  6.8 0.7 %copy-done.4 = f32[28,28]{1,0:T(8,128)S(1)} copy-done((f32[28,28]{1,0:T(8,128)S(1)}, f32[28,28]{1,0:T(8,128)}, u32[]{:S(2)}) %copy-start.4) | copy-done | bytes 3160
  7.6 0.0 copy-start.5
  7.6 0.7 %copy-done.5 = f32[28,28]{1,0:T(8,128)S(1)} copy-done((f32[28,28]{1,0:T(8,128)S(1)}, f32[28,28]{1,0:T(8,128)}, u32[]{:S(2)}) %copy-start.5) | copy-done | bytes 3160
  8.3 0.0 copy-start.6
  8.3 0.7 %copy-done.6 = f32[28,28]{1,0:T(8,128)S(1)} copy-done((f32[28,28]{1,0:T(8,128)S(1)}, f32[28,28]{1,0:T(8,128)}, u32[]{:S(2)}) %copy-start.6) | copy-done | bytes 3160
  9.0 0.0 copy-start.7
  9.0 0.7 %copy-done.7 = f32[28]{0:T(128)S(1)} copy-done((f32[28]{0:T(128)S(1)}, f32[28]{0:T(128)}, u32[]{:S(2)}) %copy-start.7) | copy-done | bytes 136
  9.6 0.0 copy-start.8
  9.6 0.7 %copy-done.8 = s32[16]{0:T(128)S(1)} copy-done((s32[16]{0:T(128)S(1)}, s32[16]{0:T(128)}, u32[]{:S(2)}) %copy-start.8) | copy-done | bytes 88
  10.3 34.5 %shard_map.122 = (bf16[3,1,14,2816]{3,2,1,0:T(8,128)(2,1)S(1)}, bf16[3,14,64,80]{3,2,1,0:T(8,128)(2,1)S(1)}) custom-call(bf16[3,14,64,80]{3,2,1,0:T(8,128)(2,1)S(1)} %bitcast.7, bf16[3,1,14,2816]{3,2,1,0:T(8,128)(2,1)S(1)} %bitcast.9, bf16[1,1408,1280]{2,1,0:T(8,128)(2,1)S(1)} %copy-done, f32[28,28]{1,0:T(8,128)S(1)} %copy-done.3, f32[28,28]{1,0:T(8,128)S(1)} %copy-done.4, ...), custom_call_target="tpu_custom_call" | custom-call | flops 1000000000 | bytes 8000000 | tf_op jit(solution)/shard_map/pallas_call | solution.py:285
  44.8 0.7 %copy.16 = bf16[3,14,1,2816]{3,1,2,0:T(8,128)(2,1)} copy(bf16[3,14,1,2816]{3,1,2,0:T(8,128)(2,1)S(1)} %bitcast.10) | data formatting | bytes 473088
  45.6 0.8 %copy.17 = bf16[3,14,80,64]{2,3,1,0:T(8,128)(2,1)} copy(bf16[3,14,80,64]{2,3,1,0:T(8,128)(2,1)S(1)} %bitcast.8) | data formatting | bytes 860160
  (2 shorter events, 0.0 us)
Async XLA Ops:
  2.0 2.0 %copy-start = (bf16[1,1408,1280]{2,1,0:T(8,128)(2,1)S(1)}, bf16[1,1408,1280]{2,1,0:T(8,128)(2,1)}, u32[]{:S(2)}) copy-start(bf16[1,1408,1280]{2,1,0:T(8,128)(2,1)} %leg_hbm.1) | copy-start | bytes 10813444
  4.1 1.1 %copy-start.1 = (bf16[3,14,80,64]{2,3,1,0:T(8,128)(2,1)S(1)}, bf16[3,14,80,64]{2,3,1,0:T(8,128)(2,1)}, u32[]{:S(2)}) copy-start(bf16[3,14,80,64]{2,3,1,0:T(8,128)(2,1)} %param.11) | copy-start | bytes 1290244
  5.2 1.0 %copy-start.2 = (bf16[3,14,1,2816]{3,1,2,0:T(8,128)(2,1)S(1)}, bf16[3,14,1,2816]{3,1,2,0:T(8,128)(2,1)}, u32[]{:S(2)}) copy-start(bf16[3,14,1,2816]{3,1,2,0:T(8,128)(2,1)} %param.12) | copy-start | bytes 709636
  6.1 0.7 %copy-start.3 = (f32[28,28]{1,0:T(8,128)S(1)}, f32[28,28]{1,0:T(8,128)}, u32[]{:S(2)}) copy-start(f32[28,28]{1,0:T(8,128)} %g_ref.1) | copy-start | bytes 9412
  6.8 0.7 %copy-start.4 = (f32[28,28]{1,0:T(8,128)S(1)}, f32[28,28]{1,0:T(8,128)}, u32[]{:S(2)}) copy-start(f32[28,28]{1,0:T(8,128)} %mi_ref.1) | copy-start | bytes 9412
  7.6 0.7 %copy-start.5 = (f32[28,28]{1,0:T(8,128)S(1)}, f32[28,28]{1,0:T(8,128)}, u32[]{:S(2)}) copy-start(f32[28,28]{1,0:T(8,128)} %mo_ref.1) | copy-start | bytes 9412
  8.3 0.7 %copy-start.6 = (f32[28,28]{1,0:T(8,128)S(1)}, f32[28,28]{1,0:T(8,128)}, u32[]{:S(2)}) copy-start(f32[28,28]{1,0:T(8,128)} %mh_ref.1) | copy-start | bytes 9412
  9.0 0.7 %copy-start.7 = (f32[28]{0:T(128)S(1)}, f32[28]{0:T(128)}, u32[]{:S(2)}) copy-start(f32[28]{0:T(128)} %param.18) | copy-start | bytes 340
  9.6 0.7 %copy-start.8 = (s32[16]{0:T(128)S(1)}, s32[16]{0:T(128)}, u32[]{:S(2)}) copy-start(s32[16]{0:T(128)} %pid_ref.1) | copy-start | bytes 196

commit v2 on v1

--- a/solution.py
+++ b/solution.py
@@ -41,10 +41,11 @@
 
 
 def kernel(
-    n, nlev, x_ref, old_ref, leg_hbm, g_ref, mi_ref, mo_ref, mh_ref, rates_ref, pid_ref, lat_ref, lim_ref,
+    n, nlev, x_hbm, old_hbm, leg_hbm, g_hbm, mi_hbm, mo_hbm, mh_hbm, rates_hbm, pid_hbm, lat_hbm, lim_hbm,
     spec_ref, out_ref,
-    leg, send1, recv1, send2, recv2, es1, er1, es2, er2,
-    leg_sem, s1, r1, s2, r2, es, er,
+    x_ref, old_ref, leg, g_ref, mi_ref, mo_ref, mh_ref, rates_ref, pid_ref, lat_ref, lim_ref,
+    send1, recv1, send2, recv2, es1, er1, es2, er2,
+    in_sem, s1, r1, s2, r2, es, er,
 ):
     lev_n = x_ref.shape[1]
     fl_n = x_ref.shape[0] * lev_n
@@ -61,8 +62,13 @@
     me, lev = lax.axis_index("wave"), lax.axis_index("lev")
     other = lax.rem(lev + 1, nlev)
 
-    leg_copy = pltpu.make_async_copy(leg_hbm.at[0], leg, leg_sem)
-    leg_copy.start()
+    pairs = [
+        (pid_hbm, pid_ref), (lat_hbm, lat_ref), (lim_hbm, lim_ref), (x_hbm, x_ref), (g_hbm, g_ref), (mi_hbm, mi_ref),
+        (mo_hbm, mo_ref), (mh_hbm, mh_ref), (rates_hbm, rates_ref), (old_hbm, old_ref), (leg_hbm.at[0], leg),
+    ]
+    loads = [pltpu.make_async_copy(src, dst, in_sem.at[i]) for i, (src, dst) in enumerate(pairs)]
+    for load in loads:
+        load.start()
 
     barrier = pltpu.get_barrier_semaphore()
 
@@ -73,9 +79,12 @@
     lax.fori_loop(1, n, greet, 0)
     pl.semaphore_signal(barrier, inc=1, device_id=(me, other), device_id_type=MESH)
 
+    for load in loads[:4]:
+        load.wait()
+
     col = iota((jl, nlat), 1)
-    own = jnp.sum(jnp.where(col == me * jl + iota((jl, nlat), 0), lat_ref[...], 0.0), axis=1, keepdims=True)
-    lim = jnp.sum(jnp.where(col.astype(F32) == own, lim_ref[...], 0.0), axis=1, keepdims=True)
+    own = jnp.sum(jnp.where(col == me * jl + iota((jl, nlat), 0), lat_ref[...].astype(F32)[None, :], 0.0), axis=1, keepdims=True)
+    lim = jnp.sum(jnp.where(col.astype(F32) == own, lim_ref[...].astype(F32)[None, :], 0.0), axis=1, keepdims=True)
     lim = jnp.sum(jnp.where(iota((jl, jl), 0) == iota((jl, jl), 1), lim, 0.0), axis=0, keepdims=True)
     q = iota((q_n, jl), 0)
     slot = q // 4
@@ -118,6 +127,8 @@
     lax.fori_loop(1, n, start1, 0)
     recv1[me] = send1[me]
 
+    for load in loads[4:10]:
+        load.wait()
     a = pid_ref[me]
     r = iota((1, nr), 1)
     first_pad = (MMAX - a + BLOCK - 1) // BLOCK * BLOCK
@@ -155,7 +166,7 @@
     w1 = jnp.concatenate([w_div, w_heat], axis=0)
     im, om = iota((half, levels), 0), iota((half, levels), 1)
     own_mode = (om == lev_n * lev + im // 2) & (im < 2 * lev_n)
-    rates = jnp.sum(jnp.where(own_mode, rates_ref[...], 0.0), axis=1, keepdims=True)
+    rates = jnp.sum(jnp.where(own_mode, rates_ref[...][None, :], 0.0), axis=1, keepdims=True)
     i2, l2 = iota((2 * mid, levels), 0), iota((2 * mid, levels), 1)
     field, level, cc = mid_row(i2 % mid)
     pick_lev = onehot(l2 == lev_n * ((lev + i2 // mid) % nlev) + level, F32)
@@ -168,7 +179,7 @@
     field, level, cc = mid_row(iota((mid, 1), 0))
     stays = onehot(field != 1, F32)
 
-    leg_copy.wait()
+    loads[10].wait()
 
     def wait1(i, carry):
         copy1(i).wait_send()
@@ -288,11 +299,20 @@
             jax.ShapeDtypeStruct((fields, 1, lev_n, 2 * nr), BF16),
             jax.ShapeDtypeStruct((fields, lev_n, q_n, jl), BF16),
         ),
-        in_specs=[vmem, vmem, pl.BlockSpec(memory_space=pl.ANY)] + [vmem] * 5
-        + [pl.BlockSpec(memory_space=pltpu.SMEM)] + [vmem] * 2,
+        in_specs=[pl.BlockSpec(memory_space=pltpu.HBM)] * 11,
         out_specs=(vmem, vmem),
         scratch_shapes=[
+            pltpu.VMEM((fields, lev_n, q_n, jl), BF16),
+            pltpu.VMEM((fields, 1, lev_n, 2 * nr), BF16),
             pltpu.VMEM((nr, nlat), BF16),
+            pltpu.VMEM(g_matrix.shape, F32),
+            pltpu.VMEM(g_matrix.shape, F32),
+            pltpu.VMEM(g_matrix.shape, F32),
+            pltpu.VMEM(g_matrix.shape, F32),
+            pltpu.VMEM(mode_rates.shape, F32),
+            pltpu.SMEM(pair_ids.shape, jnp.int32),
+            pltpu.VMEM(lat_ids.shape, jnp.int32),
+            pltpu.VMEM(limits.shape, jnp.int32),
             pltpu.VMEM((n, 16, lanes), BF16),
             pltpu.VMEM((n, 16, lanes), BF16),
             pltpu.VMEM((n, 16, lanes), BF16),
@@ -301,7 +321,7 @@
             pltpu.VMEM((half, nr), BF16),
             pltpu.VMEM((mid, nr), BF16),
             pltpu.VMEM((mid, nr), BF16),
-            pltpu.SemaphoreType.DMA,
+            pltpu.SemaphoreType.DMA((11,)),
             pltpu.SemaphoreType.DMA((n,)),
             pltpu.SemaphoreType.DMA((n,)),
             pltpu.SemaphoreType.DMA((n,)),
@@ -310,7 +330,7 @@
             pltpu.SemaphoreType.DMA((2,)),
         ],
         compiler_params=pltpu.CompilerParams(
-            collective_id=0, has_side_effects=True, vmem_limit_bytes=48 * 1024 * 1024
+            collective_id=0, has_side_effects=True, vmem_limit_bytes=63 * 1024 * 1024
         ),
         cost_estimate=pl.CostEstimate(flops=10**9, bytes_accessed=8 * 10**6, transcendentals=0),
     )(
@@ -321,10 +341,10 @@
         modes_in,
         modes_out,
         mode_heating,
-        mode_rates[None, :],
+        mode_rates,
         pair_ids,
-        lat_ids.astype(F32)[None, :],
-        limits.astype(F32)[None, :],
+        lat_ids,
+        limits,
     )
     return jnp.transpose(spec, (0, 2, 1, 3)), jnp.transpose(out, (0, 1, 3, 2))
 

time: 47.1 us -> 39 us (0.83)
  local copies, waits for them, and re-layouts: 9.82 us -> 3.67 us
  other arithmetic: 1.4 us -> 0 us
    unnamed x20 -> x2, local copies, waits for them, and re-layouts: 9.8 us -> 3.67 us
    convert_element_type x2 -> x0, other arithmetic: 1.4 us -> none  [the longest x1 0.7 us: body(): lat_ids.astype(F32)[None, :]]
where the time goes in v2:
time: 39 us; the launch traced here: 38.8 us
  Pallas kernels  34.5 us (88%)
  local copies, waits for them, and re-layouts  3.67 us (9%)
  between operations  0.64 us (2%)
    pallas_call x1, Pallas kernels, body(): pl.pallas_call(functools.partial(kernel, n, nlev), out_shape=(jax.ShapeDt...  34.5 us
    unnamed x2, local copies, waits for them, and re-layouts  3.67 us

profile of v2, /device:TPU:28, one launch (start us, length us, event | category | flops | bytes accessed | tf_op | source)
XLA Modules:
  0.0 38.8 jit_solution(5289549941504726533)
XLA Ops:
  0.6 34.5 %shard_map.122 = (bf16[3,1,14,2816]{3,2,1,0:T(8,128)(2,1)}, bf16[3,14,64,80]{3,2,1,0:T(8,128)(2,1)}) custom-call(bf16[3,14,64,80]{3,2,1,0:T(8,128)(2,1)} %bitcast.6, bf16[3,1,14,2816]{3,2,1,0:T(8,128)(2,1)} %bitcast.8, bf16[1,1408,1280]{2,1,0:T(8,128)(2,1)} %leg_hbm.1, f32[28,28]{1,0:T(8,128)} %g_hbm.1, f32[28,28]{1,0:T(8,128)} %mi_hbm.1, f32[28,28]{1,0:T(8,128)} %mo_hbm.1, ...), custom_call_target="tpu_custom_call" | custom-call | flops 1000000000 | bytes 8000000 | tf_op jit(solution)/shard_map/pallas_call | solution.py:296
  35.1 1.7 %copy.16 = bf16[3,14,1,2816]{3,1,2,0:T(8,128)(2,1)} copy(bf16[3,14,1,2816]{3,1,2,0:T(8,128)(2,1)} %bitcast.9) | data formatting | bytes 473088
  36.8 2.0 %copy.17 = bf16[3,14,80,64]{2,3,1,0:T(8,128)(2,1)} copy(bf16[3,14,80,64]{2,3,1,0:T(8,128)(2,1)} %bitcast.7) | data formatting | bytes 860160

commit v3 on v2

--- a/solution.py
+++ b/solution.py
@@ -42,10 +42,10 @@
 
 def kernel(
     n, nlev, x_hbm, old_hbm, leg_hbm, g_hbm, mi_hbm, mo_hbm, mh_hbm, rates_hbm, pid_hbm, lat_hbm, lim_hbm,
-    spec_ref, out_ref,
-    x_ref, old_ref, leg, g_ref, mi_ref, mo_ref, mh_ref, rates_ref, pid_ref, lat_ref, lim_ref,
+    spec_hbm, out_hbm,
+    spec_ref, out_ref, x_ref, old_ref, leg, g_ref, mi_ref, mo_ref, mh_ref, rates_ref, pid_ref, lat_ref, lim_ref,
     send1, recv1, send2, recv2, es1, er1, es2, er2,
-    in_sem, s1, r1, s2, r2, es, er,
+    out_sem, in_sem, s1, r1, s2, r2, es, er,
 ):
     lev_n = x_ref.shape[1]
     fl_n = x_ref.shape[0] * lev_n
@@ -113,18 +113,27 @@
 
     pl.semaphore_wait(barrier, n)
 
-    def copy1(i):
-        to = lax.rem(me + i, n)
+    hn = n // 2
+    near, far = me // hn, 1 - me // hn
+
+    def peer(side, i):
+        return side * hn + lax.rem(me + i, hn)
+
+    def copy1(to):
         return pltpu.make_async_remote_copy(
             src_ref=send1.at[to], dst_ref=recv1.at[me], send_sem=s1.at[to], recv_sem=r1.at[me],
             device_id=(to, lev), device_id_type=MESH,
         )
 
-    def start1(i, carry):
-        copy1(i).start()
-        return carry
-
-    lax.fori_loop(1, n, start1, 0)
+    def start1(side):
+        def step(i, carry):
+            copy1(peer(side, i)).start()
+            return carry
+
+        return step
+
+    lax.fori_loop(0, hn, start1(far), 0)
+    lax.fori_loop(1, hn, start1(near), 0)
     recv1[me] = send1[me]
 
     for load in loads[4:10]:
@@ -181,25 +190,31 @@
 
     loads[10].wait()
 
-    def wait1(i, carry):
-        copy1(i).wait_send()
-        frm = lax.rem(me + n - i, n)
-        pltpu.make_async_remote_copy(
-            src_ref=send1.at[frm], dst_ref=recv1.at[frm], send_sem=s1.at[frm], recv_sem=r1.at[frm],
-            device_id=(frm, lev), device_id_type=MESH,
-        ).wait_recv()
-        return carry
-
-    lax.fori_loop(1, n, wait1, 0)
-
-    cols = jnp.concatenate(
-        [
-            jnp.concatenate([recv1[d, :, g * jl : (g + 1) * jl] for d in range(n)], axis=1)
-            for g in range(groups)
-        ],
-        axis=0,
-    )
-    both = lax.dot_general(cols, leg[...], NT, preferred_element_type=F32).reshape(groups, 2, 8, nr)
+    def wait1(side):
+        def step(i, carry):
+            frm = peer(side, i)
+            pltpu.make_async_remote_copy(
+                src_ref=send1.at[frm], dst_ref=recv1.at[frm], send_sem=s1.at[frm], recv_sem=r1.at[frm],
+                device_id=(frm, lev), device_id_type=MESH,
+            ).wait_recv()
+            return carry
+
+        return step
+
+    def lat_half(side):
+        return pl.ds(pl.multiple_of(side * (hn * jl), 128), hn * jl)
+
+    def forward(side):
+        got = [recv1[side * hn + d] for d in range(hn)]
+        cols = jnp.concatenate(
+            [jnp.concatenate([m[:, g * jl : (g + 1) * jl] for m in got], axis=1) for g in range(groups)], axis=0
+        )
+        return lax.dot_general(cols, leg[:, lat_half(side)], NT, preferred_element_type=F32)
+
+    lax.fori_loop(1, hn, wait1(near), 0)
+    both = forward(near)
+    lax.fori_loop(0, hn, wait1(far), 0)
+    both = (both + forward(far)).reshape(groups, 2, 8, nr)
     total = jnp.where(iota((groups, 8, nr), 2) < first_pad, both[:, 0], both[:, 1])
     total = old_rows + jnp.where(used, total.reshape(trows, nr), 0.0)
 
@@ -232,25 +247,28 @@
         ],
         axis=1,
     ).reshape(rows, nr).astype(BF16)
-    grid = dot(sides, leg[...]).astype(BF16)
-    for d in range(n):
-        parts = [grid[g * 16 : (g + 1) * 16, d * jl : (d + 1) * jl] for g in range(groups)]
-        if lanes > groups * jl:
-            parts.append(jnp.zeros((16, lanes - groups * jl), BF16))
-        send2[d] = jnp.concatenate(parts, axis=1)
-
-    def copy2(i):
-        to = lax.rem(me + i, n)
+
+    def copy2(to):
         return pltpu.make_async_remote_copy(
             src_ref=send2.at[to], dst_ref=recv2.at[me], send_sem=s2.at[to], recv_sem=r2.at[me],
             device_id=(to, lev), device_id_type=MESH,
         )
 
-    def start2(i, carry):
-        copy2(i).start()
-        return carry
-
-    lax.fori_loop(1, n, start2, 0)
+    def start2(side):
+        def step(i, carry):
+            copy2(peer(side, i)).start()
+            return carry
+
+        return step
+
+    for side, begin in ((far, 0), (near, 1)):
+        grid = dot(sides, leg[:, lat_half(side)]).astype(BF16)
+        for d in range(hn):
+            parts = [grid[g * 16 : (g + 1) * 16, d * jl : (d + 1) * jl] for g in range(groups)]
+            if lanes > groups * jl:
+                parts.append(jnp.zeros((16, lanes - groups * jl), BF16))
+            send2[side * hn + d] = jnp.concatenate(parts, axis=1)
+        lax.fori_loop(begin, hn, start2(side), 0)
     recv2[me] = send2[me]
 
     new_b = new.astype(BF16)
@@ -261,8 +279,13 @@
         for f in range(3):
             spec_ref[f, 0, :, c * nr : (c + 1) * nr] = part[f * lev_n : (f + 1) * lev_n]
 
+    spec_copy = pltpu.make_async_copy(spec_ref, spec_hbm, out_sem.at[0])
+    spec_copy.start()
+
     def wait2(i, carry):
-        copy2(i).wait_send()
+        to = lax.rem(me + i, n)
+        copy1(to).wait_send()
+        copy2(to).wait_send()
         frm = lax.rem(me + n - i, n)
         pltpu.make_async_remote_copy(
             src_ref=send2.at[frm], dst_ref=recv2.at[frm], send_sem=s2.at[frm], recv_sem=r2.at[frm],
@@ -271,6 +294,7 @@
         return carry
 
     lax.fori_loop(1, n, wait2, 0)
+    out_copies = []
     perm_back = onehot(pr == pc % K * q_n + pc // K)
     back = dot(perm_back, recv2[...].reshape(K * q_n, lanes))
     for g in range(groups):
@@ -279,6 +303,13 @@
             if fl < fl_n:
                 piece = back[k * q_n : (k + 1) * q_n, g * jl : (g + 1) * jl] * keep
                 out_ref[fl // lev_n, fl % lev_n] = piece.astype(BF16)
+                if fl % lev_n == lev_n - 1:
+                    f = fl // lev_n
+                    out_copies.append(pltpu.make_async_copy(out_ref.at[f], out_hbm.at[f], out_sem.at[1 + f]))
+                    out_copies[-1].start()
+    spec_copy.wait()
+    for out_copy in out_copies:
+        out_copy.wait()
 
 
 def body(
@@ -292,16 +323,18 @@
     nr, nlat = legendre.shape[1:]
     half = (2 * lev_n + 15) // 16 * 16
     mid = groups * 8 - lev_n // K * 8
-    vmem = pl.BlockSpec(memory_space=pltpu.VMEM)
+    hbm = pl.BlockSpec(memory_space=pltpu.HBM)
     spec, out = pl.pallas_call(
         functools.partial(kernel, n, nlev),
         out_shape=(
             jax.ShapeDtypeStruct((fields, 1, lev_n, 2 * nr), BF16),
             jax.ShapeDtypeStruct((fields, lev_n, q_n, jl), BF16),
         ),
-        in_specs=[pl.BlockSpec(memory_space=pltpu.HBM)] * 11,
-        out_specs=(vmem, vmem),
+        in_specs=[hbm] * 11,
+        out_specs=(hbm, hbm),
         scratch_shapes=[
+            pltpu.VMEM((fields, 1, lev_n, 2 * nr), BF16),
+            pltpu.VMEM((fields, lev_n, q_n, jl), BF16),
             pltpu.VMEM((fields, lev_n, q_n, jl), BF16),
             pltpu.VMEM((fields, 1, lev_n, 2 * nr), BF16),
             pltpu.VMEM((nr, nlat), BF16),
@@ -321,6 +354,7 @@
             pltpu.VMEM((half, nr), BF16),
             pltpu.VMEM((mid, nr), BF16),
             pltpu.VMEM((mid, nr), BF16),
+            pltpu.SemaphoreType.DMA((1 + fields,)),
             pltpu.SemaphoreType.DMA((11,)),
             pltpu.SemaphoreType.DMA((n,)),
             pltpu.SemaphoreType.DMA((n,)),

time: 39 us -> 41.9 us (1.074)
  the two profiles are of different devices: /device:TPU:28 before, /device:TPU:0 now
where the time goes in v3:
time: 41.9 us; the launch traced here: 41.7 us
  Pallas kernels  37.4 us (89%)
  local copies, waits for them, and re-layouts  3.67 us (9%)
  between operations  0.64 us (2%)
    pallas_call x1, Pallas kernels, body(): pl.pallas_call(functools.partial(kernel, n, nlev), out_shape=(jax.ShapeDt...  37.4 us
    unnamed x2, local copies, waits for them, and re-layouts  3.67 us

profile of v3, /device:TPU:0, one launch (start us, length us, event | category | flops | bytes accessed | tf_op | source)
XLA Modules:
  0.0 41.7 jit_solution(8956782389613698681)
XLA Ops:
  0.6 37.4 %shard_map.122 = (bf16[3,1,14,2816]{3,2,1,0:T(8,128)(2,1)}, bf16[3,14,64,80]{3,2,1,0:T(8,128)(2,1)}) custom-call(bf16[3,14,64,80]{3,2,1,0:T(8,128)(2,1)} %bitcast.6, bf16[3,1,14,2816]{3,2,1,0:T(8,128)(2,1)} %bitcast.8, bf16[1,1408,1280]{2,1,0:T(8,128)(2,1)} %leg_hbm.1, f32[28,28]{1,0:T(8,128)} %g_hbm.1, f32[28,28]{1,0:T(8,128)} %mi_hbm.1, f32[28,28]{1,0:T(8,128)} %mo_hbm.1, ...), custom_call_target="tpu_custom_call" | custom-call | flops 1000000000 | bytes 8000000 | tf_op jit(solution)/shard_map/pallas_call | solution.py:327
  38.0 1.7 %copy.16 = bf16[3,14,1,2816]{3,1,2,0:T(8,128)(2,1)} copy(bf16[3,14,1,2816]{3,1,2,0:T(8,128)(2,1)} %bitcast.9) | data formatting | bytes 473088
  39.7 2.0 %copy.17 = bf16[3,14,80,64]{2,3,1,0:T(8,128)(2,1)} copy(bf16[3,14,80,64]{2,3,1,0:T(8,128)(2,1)} %bitcast.7) | data formatting | bytes 860160

commit v4 on v2

--- a/solution.py
+++ b/solution.py
@@ -42,10 +42,10 @@
 
 def kernel(
     n, nlev, x_hbm, old_hbm, leg_hbm, g_hbm, mi_hbm, mo_hbm, mh_hbm, rates_hbm, pid_hbm, lat_hbm, lim_hbm,
-    spec_ref, out_ref,
-    x_ref, old_ref, leg, g_ref, mi_ref, mo_ref, mh_ref, rates_ref, pid_ref, lat_ref, lim_ref,
+    spec_hbm, out_hbm,
+    spec_ref, out_ref, x_ref, old_ref, leg, g_ref, mi_ref, mo_ref, mh_ref, rates_ref, pid_ref, lat_ref, lim_ref,
     send1, recv1, send2, recv2, es1, er1, es2, er2,
-    in_sem, s1, r1, s2, r2, es, er,
+    out_sem, in_sem, s1, r1, s2, r2, es, er,
 ):
     lev_n = x_ref.shape[1]
     fl_n = x_ref.shape[0] * lev_n
@@ -182,7 +182,6 @@
     loads[10].wait()
 
     def wait1(i, carry):
-        copy1(i).wait_send()
         frm = lax.rem(me + n - i, n)
         pltpu.make_async_remote_copy(
             src_ref=send1.at[frm], dst_ref=recv1.at[frm], send_sem=s1.at[frm], recv_sem=r1.at[frm],
@@ -261,7 +260,11 @@
         for f in range(3):
             spec_ref[f, 0, :, c * nr : (c + 1) * nr] = part[f * lev_n : (f + 1) * lev_n]
 
+    spec_copy = pltpu.make_async_copy(spec_ref, spec_hbm, out_sem.at[0])
+    spec_copy.start()
+
     def wait2(i, carry):
+        copy1(i).wait_send()
         copy2(i).wait_send()
         frm = lax.rem(me + n - i, n)
         pltpu.make_async_remote_copy(
@@ -271,6 +274,7 @@
         return carry
 
     lax.fori_loop(1, n, wait2, 0)
+    out_copies = []
     perm_back = onehot(pr == pc % K * q_n + pc // K)
     back = dot(perm_back, recv2[...].reshape(K * q_n, lanes))
     for g in range(groups):
@@ -279,6 +283,13 @@
             if fl < fl_n:
                 piece = back[k * q_n : (k + 1) * q_n, g * jl : (g + 1) * jl] * keep
                 out_ref[fl // lev_n, fl % lev_n] = piece.astype(BF16)
+                if fl % lev_n == lev_n - 1:
+                    f = fl // lev_n
+                    out_copies.append(pltpu.make_async_copy(out_ref.at[f], out_hbm.at[f], out_sem.at[1 + f]))
+                    out_copies[-1].start()
+    spec_copy.wait()
+    for out_copy in out_copies:
+        out_copy.wait()
 
 
 def body(
@@ -292,16 +303,18 @@
     nr, nlat = legendre.shape[1:]
     half = (2 * lev_n + 15) // 16 * 16
     mid = groups * 8 - lev_n // K * 8
-    vmem = pl.BlockSpec(memory_space=pltpu.VMEM)
+    hbm = pl.BlockSpec(memory_space=pltpu.HBM)
     spec, out = pl.pallas_call(
         functools.partial(kernel, n, nlev),
         out_shape=(
             jax.ShapeDtypeStruct((fields, 1, lev_n, 2 * nr), BF16),
             jax.ShapeDtypeStruct((fields, lev_n, q_n, jl), BF16),
         ),
-        in_specs=[pl.BlockSpec(memory_space=pltpu.HBM)] * 11,
-        out_specs=(vmem, vmem),
+        in_specs=[hbm] * 11,
+        out_specs=(hbm, hbm),
         scratch_shapes=[
+            pltpu.VMEM((fields, 1, lev_n, 2 * nr), BF16),
+            pltpu.VMEM((fields, lev_n, q_n, jl), BF16),
             pltpu.VMEM((fields, lev_n, q_n, jl), BF16),
             pltpu.VMEM((fields, 1, lev_n, 2 * nr), BF16),
             pltpu.VMEM((nr, nlat), BF16),
@@ -321,6 +334,7 @@
             pltpu.VMEM((half, nr), BF16),
             pltpu.VMEM((mid, nr), BF16),
             pltpu.VMEM((mid, nr), BF16),
+            pltpu.SemaphoreType.DMA((1 + fields,)),
             pltpu.SemaphoreType.DMA((11,)),
             pltpu.SemaphoreType.DMA((n,)),
             pltpu.SemaphoreType.DMA((n,)),

time: 39 us -> 38.9 us (level)
  no operation moved by 1% of the time
where the time goes in v4:
time: 38.9 us; the launch traced here: 38.7 us
  Pallas kernels  34.4 us (88%)
  local copies, waits for them, and re-layouts  3.67 us (9%)
  between operations  0.64 us (2%)
    pallas_call x1, Pallas kernels, body(): pl.pallas_call(functools.partial(kernel, n, nlev), out_shape=(jax.ShapeDt...  34.4 us
    unnamed x2, local copies, waits for them, and re-layouts  3.67 us

profile of v4, /device:TPU:28, one launch (start us, length us, event | category | flops | bytes accessed | tf_op | source)
XLA Modules:
  0.0 38.7 jit_solution(11104258362064965793)
XLA Ops:
  0.6 34.4 %shard_map.122 = (bf16[3,1,14,2816]{3,2,1,0:T(8,128)(2,1)}, bf16[3,14,64,80]{3,2,1,0:T(8,128)(2,1)}) custom-call(bf16[3,14,64,80]{3,2,1,0:T(8,128)(2,1)} %bitcast.6, bf16[3,1,14,2816]{3,2,1,0:T(8,128)(2,1)} %bitcast.8, bf16[1,1408,1280]{2,1,0:T(8,128)(2,1)} %leg_hbm.1, f32[28,28]{1,0:T(8,128)} %g_hbm.1, f32[28,28]{1,0:T(8,128)} %mi_hbm.1, f32[28,28]{1,0:T(8,128)} %mo_hbm.1, ...), custom_call_target="tpu_custom_call" | custom-call | flops 1000000000 | bytes 8000000 | tf_op jit(solution)/shard_map/pallas_call | solution.py:307
  35.0 1.7 %copy.16 = bf16[3,14,1,2816]{3,1,2,0:T(8,128)(2,1)} copy(bf16[3,14,1,2816]{3,1,2,0:T(8,128)(2,1)} %bitcast.9) | data formatting | bytes 473088
  36.7 2.0 %copy.17 = bf16[3,14,80,64]{2,3,1,0:T(8,128)(2,1)} copy(bf16[3,14,80,64]{2,3,1,0:T(8,128)(2,1)} %bitcast.7) | data formatting | bytes 860160
